TPU v7x, 128 devices: a whole 4x4x4 slice. The times are simulated.
128 devices in a mesh: gx: 8 (over x, core), gy: 16 (over y, z).
Axes of the slice: x: 4, y: 4, z: 4, core: 2. Of those that a mesh axis runs over, the one named last changes fastest.
Arguments:
- ocean_state: float32 [4, 16, 768, 2304], P(None, None, 'gy', 'gx'), may hold values from -8 to 8, as said below
- layer_thickness: float32 [16], replicated, may hold values from 0.05 to 0.3
- vertical_mixing: float32 [768, 2304], P('gy', 'gx'), may hold values from 0.1 to 10
- damping: float32 [768, 2304], P('gy', 'gx'), may hold values from 0.02 to 3
- ocean_blocks: int32 [32, 64], replicated, may hold values from 0 to 1, as said below
Outputs:
- tracer_next: float32 [2, 16, 768, 2304], P(None, None, 'gy', 'gx')
- surface_height: float32 [768, 2304], P('gy', 'gx')
Inputs may be any that keep to these rules, and one draw needn't show every extreme that they name: `ocean_state`: the first two components are temperature and salinity, the last two the eastward and northward velocity. `ocean_blocks`: each device's patch of 2 x 8 blocks (latitude rows from j * 2, longitude columns from i * 8, for gy index j and gx index i) holds 3 to 16 ocean blocks; in every draw some patch and the patches on both sides of it along latitude are wholly ocean, and a patch next to that run of three along latitude holds exactly 3.
All inputs are finite; a program needn't handle non-finite values.
Results may differ from a plain program's by a relative error of at most 0.0003.
Values sent between devices are 32-bit elements; how exact they have to be, the bound alone decides.
A program may use at most 64 MiB of HBM per device.

v0:
```python
import jax
import jax.numpy as jnp
import numpy as np
from jax import lax
from jax.sharding import PartitionSpec as P

BLAT = 24
BLON = 36
ITERS = 4


advect_rate = 0.2
diffuse_rate = 0.1
salt_weight = 0.5


def extended_2(array, sides, width, wrap):
    for axis, dim in sides:
        devices, length = (lax.axis_size(axis), array.shape[dim])
        up = [(i, (i + 1) % devices) for i in range(devices if wrap else devices - 1)]
        down = [(j, i) for i, j in up]
        last = lax.slice_in_dim(array, length - width, length, axis=dim)
        first = lax.slice_in_dim(array, 0, width, axis=dim)
        before = lax.ppermute(last, axis, up)
        after = lax.ppermute(first, axis, down)
        array = jnp.concatenate([before, array, after], axis=dim)
    return array


def shifted(value, axis, steps):
    count = lax.axis_size(axis)
    first, last = (max(0, -steps), min(count, count - steps))
    return lax.ppermute(value, axis, [(source, source + steps) for source in range(first, last)])


def middle(field):
    return field[..., 1:-1, 1:-1]


def eastern(field):
    return field[..., 1:-1, 2:]


def western(field):
    return field[..., 1:-1, :-2]


def northern(field):
    return field[..., 2:, 1:-1]


def southern(field):
    return field[..., :-2, 1:-1]


def horizontal(fields, margin):
    tracers = fields[0:2] * margin
    east_speed = fields[2] * margin
    north_speed = fields[3] * margin
    flux_east = (
        0.25 * (middle(east_speed) + eastern(east_speed)) * (middle(tracers) + eastern(tracers))
    )
    flux_west = (
        0.25 * (western(east_speed) + middle(east_speed)) * (western(tracers) + middle(tracers))
    )
    flux_north = (
        0.25 * (middle(north_speed) + northern(north_speed)) * (middle(tracers) + northern(tracers))
    )
    flux_south = (
        0.25 * (southern(north_speed) + middle(north_speed)) * (southern(tracers) + middle(tracers))
    )
    advection = flux_east - flux_west + flux_north - flux_south
    diffusion = (
        eastern(tracers)
        + western(tracers)
        + northern(tracers)
        + southern(tracers)
        - 4.0 * middle(tracers)
    )
    return middle(margin) * (middle(tracers) - advect_rate * advection + diffuse_rate * diffusion)


def vertical_mix(advected, thickness, mixing):
    levels = advected.shape[1]
    coupling = [mixing / (thickness[level] + thickness[level + 1]) for level in range(levels - 1)]
    ratios = []
    values = []
    for level in range(levels):
        below = coupling[level - 1] if level > 0 else 0.0
        above = coupling[level] if level < levels - 1 else 0.0
        diagonal = thickness[level] + below + above
        source = thickness[level] * advected[:, level]
        if level == 0:
            denom = diagonal
            value = source / denom
        else:
            denom = diagonal - below * ratios[-1]
            value = (source + below * values[-1]) / denom
        ratios.append(above / denom)
        values.append(value)
    result = [values[-1]]
    for level in range(levels - 2, -1, -1):
        result.insert(0, values[level] + ratios[level] * result[0])
    return jnp.stack(result, axis=1)


def nine_point(frame, diagonal):
    edges = northern(frame) + southern(frame) + eastern(frame) + western(frame)
    corners = frame[..., 2:, 2:] + frame[..., 2:, :-2] + frame[..., :-2, 2:] + frame[..., :-2, :-2]
    return diagonal * middle(frame) - edges - 0.5 * corners


def static_tables(lat_cells, lon_cells):
    interior = lat_cells * lon_cells
    rim_rows = np.concatenate(
        [
            np.zeros(lon_cells),
            np.full(lon_cells, lat_cells - 1),
            np.arange(1, lat_cells - 1),
            np.arange(1, lat_cells - 1),
        ]
    ).astype(np.int64)
    rim_cols = np.concatenate(
        [
            np.arange(lon_cells),
            np.arange(lon_cells),
            np.zeros(lat_cells - 2),
            np.full(lat_cells - 2, lon_cells - 1),
        ]
    ).astype(np.int64)
    rim_cells = rim_rows * lon_cells + rim_cols
    rim_of_cell = np.zeros(interior, np.int64)
    rim_of_cell[rim_cells] = np.arange(rim_cells.shape[0])
    frame_rows = np.repeat(np.arange(lat_cells + 2), lon_cells + 2)
    frame_cols = np.tile(np.arange(lon_cells + 2), lat_cells + 2)
    on_cycle = (
        (frame_rows == 0)
        | (frame_rows == lat_cells + 1)
        | (frame_cols == 0)
        | (frame_cols == lon_cells + 1)
    )
    cycle_place = np.cumsum(on_cycle) - 1
    frame_source = np.where(
        on_cycle, interior + cycle_place, (frame_rows - 1) * lon_cells + (frame_cols - 1)
    )
    cycle_lat = frame_rows[on_cycle] - 1
    cycle_lon = frame_cols[on_cycle] - 1
    return (rim_cells, rim_of_cell, frame_source, cycle_lat, cycle_lon)


def blocks_of(field, lat_blocks, lon_blocks):
    shaped = field.reshape(lat_blocks, BLAT, lon_blocks, BLON).transpose(0, 2, 1, 3)
    return shaped.reshape(lat_blocks * lon_blocks, BLAT * BLON)


def field_of(blocks, lat_blocks, lon_blocks):
    shaped = blocks.reshape(lat_blocks, lon_blocks, BLAT, BLON).transpose(0, 2, 1, 3)
    return shaped.reshape(lat_blocks * BLAT, lon_blocks * BLON)


def ownership(ocean_blocks, lat_groups, lon_groups):
    block_rows, block_cols = ocean_blocks.shape
    per_lat = block_rows // lat_groups
    per_lon = block_cols // lon_groups
    patch = ocean_blocks.reshape(lat_groups, per_lat, lon_groups, per_lon).transpose(0, 2, 1, 3)
    patch = patch.reshape(lat_groups, lon_groups, per_lat * per_lon)
    before = jnp.cumsum(patch, axis=2) - patch
    totals = jnp.sum(patch, axis=2)
    upper = jnp.concatenate([totals[1:], totals[-1:]], axis=0)
    moving = (upper >= totals + 2).astype(jnp.int32) - (totals >= upper + 2).astype(jnp.int32)
    last_row = (jnp.arange(lat_groups) == lat_groups - 1)[:, None]
    shifts = jnp.where(last_row, 0, moving)
    earlier = jnp.concatenate([jnp.zeros_like(shifts[:1]), shifts[:-1]], axis=0)
    owned = totals + shifts - earlier
    owned_below = jnp.concatenate([jnp.zeros_like(owned[:1]), owned[:-1]], axis=0)
    first = (patch == 1) & (before == 0)
    final = (patch == 1) & (before == totals[:, :, None] - 1)
    owner_shift = jnp.where(
        final & (shifts[:, :, None] == -1), 1, jnp.where(first & (earlier[:, :, None] == 1), -1, 0)
    )
    own_slot = (
        before
        - (earlier[:, :, None] == 1).astype(jnp.int32)
        + (earlier[:, :, None] == -1).astype(jnp.int32)
    )
    slot = jnp.where(
        owner_shift == 1, 0, jnp.where(owner_shift == -1, owned_below[:, :, None] - 1, own_slot)
    )
    return (patch, owner_shift, slot, owned, shifts, earlier, first, final)


def to_grid(table, lat_groups, lon_groups, per_lat, per_lon):
    shaped = table.reshape(lat_groups, lon_groups, per_lat, per_lon).transpose(0, 2, 1, 3)
    return shaped.reshape(-1)


def norm_sum(first_field, second_field):
    return lax.psum(jnp.sum(first_field * second_field), ("gx", "gy"))


def curvature_sum(first_field, second_field):
    return lax.psum(jnp.sum(first_field * second_field), ("gx", "gy"))


def solve(rhs, diagonal, apply_op):
    surface = jnp.zeros_like(rhs)
    residual = rhs
    scaled = residual / diagonal
    direction = scaled
    norm_now = norm_sum(residual, scaled)
    for iteration in range(ITERS):
        image = apply_op(direction)
        step_size = norm_now / curvature_sum(direction, image)
        surface = surface + step_size * direction
        if iteration + 1 < ITERS:
            residual = residual - step_size * image
            scaled = residual / diagonal
            norm_next = norm_sum(residual, scaled)
            direction = scaled + norm_next / norm_now * direction
            norm_now = norm_next
    return surface


def body(ocean_state, layer_thickness, vertical_mixing, damping, ocean_blocks):
    lon_index = lax.axis_index("gx")
    lat_index = lax.axis_index("gy")
    lon_groups = lax.axis_size("gx")
    lat_groups = lax.axis_size("gy")
    block_rows, block_cols = ocean_blocks.shape
    per_lat = block_rows // lat_groups
    per_lon = block_cols // lon_groups
    patch_size = per_lat * per_lon
    height = per_lat * BLAT
    width = per_lon * BLON
    wrapped = jnp.concatenate([ocean_blocks[:, -1:], ocean_blocks, ocean_blocks[:, :1]], axis=1)
    wrapped = jnp.pad(wrapped, ((1, 1), (0, 0)))
    nearby = lax.dynamic_slice(
        wrapped, (lat_index * per_lat, lon_index * per_lon), (per_lat + 2, per_lon + 2)
    )
    cell_mask = jnp.repeat(jnp.repeat(nearby.astype(jnp.float32), BLAT, axis=0), BLON, axis=1)
    margin_mask = cell_mask[BLAT - 1 : BLAT + height + 1, BLON - 1 : BLON + width + 1]
    along_lon = extended_2(ocean_state, (("gx", 3),), 1, True)
    extended = extended_2(along_lon, (("gy", 2),), 1, False)
    advected = horizontal(extended, margin_mask)
    tracer_next = vertical_mix(advected, layer_thickness, vertical_mixing)
    forcing = jnp.sum(
        layer_thickness[:, None, None] * (tracer_next[0] - salt_weight * tracer_next[1]), axis=0
    )
    rim_cells, rim_of_cell, frame_source, cycle_lat, cycle_lon = static_tables(BLAT, BLON)
    rim_cells = jnp.asarray(rim_cells, jnp.int32)
    rim_of_cell = jnp.asarray(rim_of_cell, jnp.int32)
    frame_source = jnp.asarray(frame_source, jnp.int32)
    cycle_lat = jnp.asarray(cycle_lat, jnp.int32)
    cycle_lon = jnp.asarray(cycle_lon, jnp.int32)
    rim_count = rim_cells.shape[0]
    patch, owner_shift, slot, owned, shifts, earlier, first, final = ownership(
        ocean_blocks, lat_groups, lon_groups
    )
    my_patch = patch[lat_index, lon_index]
    my_shift = owner_shift[lat_index, lon_index]
    my_slot = slot[lat_index, lon_index]
    my_owned = owned[lat_index, lon_index]
    my_moving = shifts[lat_index, lon_index]
    my_earlier = earlier[lat_index, lon_index]
    positions = jnp.arange(patch_size, dtype=jnp.int32)
    lower_lat = jnp.maximum(lat_index - 1, 0)
    upper_lat = jnp.minimum(lat_index + 1, lat_groups - 1)
    first_pos = jnp.sum(positions * first[lat_index, lon_index])
    final_pos = jnp.sum(positions * final[lat_index, lon_index])
    lower_final = jnp.sum(positions * final[lower_lat, lon_index])
    upper_first = jnp.sum(positions * first[upper_lat, lon_index])
    local_blocks = jnp.stack(
        [blocks_of(forcing, per_lat, per_lon), blocks_of(damping, per_lat, per_lon)], axis=1
    )
    edge_blocks = jnp.take(local_blocks, jnp.stack([first_pos, final_pos]), axis=0)[None]
    arrived = extended_2(edge_blocks, (("gy", 0),), 1, False)
    candidates = jnp.concatenate([local_blocks, arrived[0, 1][None], arrived[2, 0][None]], axis=0)
    own_match = (
        (my_shift[None, :] == 0)
        & (my_patch[None, :] == 1)
        & (my_slot[None, :] == positions[:, None])
    )
    own_row = jnp.sum(own_match.astype(jnp.int32) * positions[None, :], axis=1)
    slot_row = jnp.where(
        (positions == 0) & (my_earlier == -1),
        patch_size,
        jnp.where((positions == my_owned - 1) & (my_moving == 1), patch_size + 1, own_row),
    )
    is_valid = positions < my_owned
    valid_float = is_valid.astype(jnp.float32)
    slot_data = jnp.take(candidates, slot_row, axis=0) * valid_float[:, None, None]
    slot_forcing = slot_data[:, 0]
    slot_diagonal = (6.0 + slot_data[:, 1]).reshape(patch_size, BLAT, BLON)
    slot_lat = jnp.where(
        slot_row == patch_size,
        (lat_index - 1) * per_lat + lower_final // per_lon,
        jnp.where(
            slot_row == patch_size + 1,
            (lat_index + 1) * per_lat + upper_first // per_lon,
            lat_index * per_lat + own_row // per_lon,
        ),
    )
    slot_lon = jnp.where(
        slot_row == patch_size,
        lon_index * per_lon + lower_final % per_lon,
        jnp.where(
            slot_row == patch_size + 1,
            lon_index * per_lon + upper_first % per_lon,
            lon_index * per_lon + own_row % per_lon,
        ),
    )
    ocean_flat = ocean_blocks.reshape(-1)
    shift_flat = to_grid(owner_shift, lat_groups, lon_groups, per_lat, per_lon)
    slot_flat = to_grid(slot, lat_groups, lon_groups, per_lat, per_lon)
    cell_rows = slot_lat[:, None] * BLAT + cycle_lat[None, :]
    cell_cols = jnp.mod(slot_lon[:, None] * BLON + cycle_lon[None, :], block_cols * BLON)
    inside = (cell_rows >= 0) & (cell_rows < block_rows * BLAT)
    cell_rows = jnp.clip(cell_rows, 0, block_rows * BLAT - 1)
    near_lat = cell_rows // BLAT
    near_lon = cell_cols // BLON
    near_flat = near_lat * block_cols + near_lon
    owner_lat = near_lat // per_lat + jnp.take(shift_flat, near_flat)
    lat_steps = owner_lat - lat_index
    lon_steps = jnp.mod(near_lon // per_lon - lon_index + 1, lon_groups) - 1
    rim_place = jnp.take(rim_of_cell, cell_rows % BLAT * BLON + cell_cols % BLON)
    cycle_source = (
        ((lon_steps + 1) * 7 + lat_steps + 3) * (patch_size * 128)
        + jnp.take(slot_flat, near_flat) * 128
        + rim_place
    )
    usable = inside & (jnp.take(ocean_flat, near_flat) == 1) & is_valid[:, None]
    cycle_source = jnp.where(usable, cycle_source, 0)
    usable_float = usable.astype(jnp.float32)

    def apply_curve(field):
        rim_values = jnp.pad(jnp.take(field, rim_cells, axis=1), ((0, 0), (0, 128 - rim_count)))
        pieces = []
        for offset in range(7):
            if offset == 3:
                pieces.append(rim_values)
            else:
                pieces.append(shifted(rim_values, "gy", 3 - offset))
        shared_lat = jnp.stack(pieces, axis=0)[None]
        shared = extended_2(shared_lat, (("gx", 0),), 1, True)
        cycle_values = jnp.take(shared.reshape(-1), cycle_source) * usable_float
        frame = jnp.take(jnp.concatenate([field, cycle_values], axis=1), frame_source, axis=1)
        frame = frame.reshape(patch_size, BLAT + 2, BLON + 2)
        return (
            nine_point(frame, slot_diagonal).reshape(patch_size, BLAT * BLON) * valid_float[:, None]
        )

    slot_surface = solve(slot_forcing, slot_diagonal.reshape(patch_size, BLAT * BLON), apply_curve)
    edge_heights = jnp.take(
        slot_surface, jnp.stack([jnp.zeros_like(my_owned), my_owned - 1]), axis=0
    )[None]
    returned = extended_2(edge_heights, (("gy", 0),), 1, False)
    home_candidates = jnp.concatenate(
        [slot_surface, returned[2, 0][None], returned[0, 1][None]], axis=0
    )
    home_row = jnp.where(
        my_shift == 0, my_slot, jnp.where(my_shift == 1, patch_size, patch_size + 1)
    )
    home_blocks = jnp.take(home_candidates, home_row, axis=0) * my_patch[:, None].astype(
        jnp.float32
    )
    surface = field_of(home_blocks, per_lat, per_lon)
    return (tracer_next, surface)


def solution(mesh):
    return jax.shard_map(
        body,
        mesh=mesh,
        in_specs=(P(None, None, "gy", "gx"), P(), P("gy", "gx"), P("gy", "gx"), P()),
        out_specs=(P(None, None, "gy", "gx"), P("gy", "gx")),
        check_vma=False,
    )
```

profile of v0, /device:TPU:1, one launch (start us, length us, event | category | flops | bytes accessed | tf_op | source)
XLA Modules:
  0.0 814.6 jit_solution(113123126408928506)
XLA Ops:
  0.6 2.4 fusion.146
  4.3 1.4 collective-permute-start.1
  9.5 2.7 reduce_window_sum.13
  23.3 3.7 fusion.129
  50.2 1.3 fusion.123
  54.2 11.6 %multiply_subtract_fusion = (f32[48,288]{1,0:T(8,128)}, f32[48,288]{1,0:T(8,128)S(1)}, f32[48,288]{1,0:T(8,128)}, f32[48,288]{1,0:T(8,128)}, f32[48,288]{1,0:T(8...) fusion(f32[]{:T(128)} %bitcast.17, ...), kind=kLoop, calls=%fused_computation.205 | loop fusion | flops 1451520 | bytes 2599036 | tf_op jit(solution)/shard_map/sub | solution.py:97
  68.2 2.5 copy.212
  70.7 2.3 pad_maximum_fusion.9
  73.0 1.4 collective-permute-start.3
  74.5 4.4 collective-permute-start.2
  78.8 1.9 compare_and_fusion.4
  81.0 3.0 pad_maximum_fusion
  85.4 1.6 fusion.7
  87.2 2.8 add_multiply_fusion
  90.4 9.3 %fusion.27 = (f32[2,1,48,288]{3,2,1,0:T(8,128)S(1)}, f32[2,1,48,288]{3,2,1,0:T(8,128)S(1)}, f32[2,1,48,288]{3,2,1,0:T(8,128)S(1)}, f32[2,1,48,288]{3,2,1,0:T(8,1...) fusion(f32[2,16,48,288]{3,2,1,0:T(8,128)S(1)} %add_multiply_fus, ...), kind=kLoop, calls=%fused_computation.94 | loop fusion | flops 1492992 | bytes 4479032 | tf_op jit(solution)/shard_map/div | solution.py:98
  99.8 2.1 add_dynamic-update-slice_fusion
  105.9 4.2 collective-permute-start.4
  113.3 1.3 collective-permute-start.10
  114.9 11.5 %gather_fusion.8 = s32[1984]{0:T(1024)S(1)} fusion(s32[2048]{0:T(1024)S(1)} %reshape.1009, s32[2048]{0:T(1024)S(1)} %pad_clamp_fusion.3), kind=kCustom, calls=%fused_computation.4.clone | custom fusion | bytes 23808 | tf_op jit(solution)/shard_map/jit(_take)/gather | solution.py:328
  126.4 11.5 %gather_fusion.6 = s32[1984]{0:T(1024)S(1)} fusion(s32[2048]{0:T(1024)S(1)} %reshape.1006, s32[2048]{0:T(1024)S(1)} %pad_clamp_fusion.3), kind=kCustom, calls=%fused_computation.clone | custom fusion | bytes 23808 | tf_op jit(solution)/shard_map/jit(_take)/gather | solution.py:331
  138.1 8.4 %gather_fusion.3 = s32[1984]{0:T(1024)S(1)} fusion(s32[864]{0:T(1024)S(1)} %copy-done, s32[2048]{0:T(1024)S(1)} %copy-done.46), kind=kCustom, calls=%fused_computation.17 | custom fusion | bytes 23808 | tf_op jit(solution)/shard_map/jit(_take)/gather | solution.py:325
  146.6 11.5 %gather_fusion.2 = s32[1984]{0:T(1024)S(1)} fusion(s32[2048]{0:T(1024)S(1)} %reshape.1008, s32[2048]{0:T(1024)S(1)} %copy-done.45), kind=kCustom, calls=%fused_computation.16 | custom fusion | bytes 23808 | tf_op jit(solution)/shard_map/jit(_take)/gather | solution.py:322
  158.2 1.3 collective-permute-start.9
  159.5 1.3 collective-permute-start.11
  160.8 4.4 collective-permute-start.8
  165.2 10.1 %collective-permute-start.7 = (f32[16,128]{0,1:T(8,128)S(1)}, f32[16,128]{0,1:T(8,128)S(1)}, u32[]{:S(2)}, u32[]{:S(2)}) collective-permute-start(f32[16,128]{0,1:T(8,128)S(1)} %get-tuple-element.130), channel_id=1, source_target_pairs={{0,2},{1,3},{2,4},{3,5},{4,6},{5,7},{6,8},{7,9},{8,10},{9,11},{10,... | collective-permute-start | bytes 24584 | tf_op jit(solution)/shard_map/ppermute | solution.py:33
  175.3 7.1 collective-permute-start.6
  184.2 4.6 collective-permute-start.13
  189.3 1.7 collective-permute-done.13
  191.0 11.5 %gather_fusion.9 = f32[1984]{0:T(1024)S(1)} fusion(f32[43008]{0:T(1024)S(1)} %bitcast.200, s32[2048]{0:T(1024)S(1)} %pad_clamp_fusion), kind=kCustom, calls=%fused_computation.2.clone | custom fusion | bytes 23808 | tf_op jit(solution)/shard_map/jit(_take)/gather | solution.py:345
  202.9 2.9 gather_fusion.10
  207.4 68.2 %all-reduce.7 = (f32[]{:T(128)}, f32[]{:T(128)}) all-reduce(f32[]{:T(128)} %get-tuple-element.11, f32[]{:T(128)} %get-tuple-element.10), channel_id=1, replica_groups=mesh['gx'=8,'gy'=16] {'gx','gy'}, use_global_device_ids=true, to_apply=%region_7.8 | all-reduce | flops 2 | bytes 16 | tf_op jit(solution)/shard_map/psum | solution.py:198
  277.5 64.2 %psum.58 = f32[]{:T(128)} all-reduce(f32[]{:T(128)} %get-tuple-element.23), channel_id=1, replica_groups=mesh['gx'=8,'gy'=16] {'gx','gy'}, use_global_device_ids=true, to_apply=%region_13.18 | all-reduce | flops 1 | bytes 8 | tf_op jit(solution)/shard_map/psum | solution.py:198
  344.0 1.3 collective-permute-start.18
  345.3 1.3 collective-permute-start.17
  347.9 4.0 collective-permute-start.16
  351.9 6.1 collective-permute-start.15
  358.1 4.9 collective-permute-start.14
  364.4 3.4 collective-permute-start.21
  369.0 11.5 %gather_fusion.12 = f32[1984]{0:T(1024)S(1)} fusion(f32[43008]{0:T(1024)S(1)} %bitcast.201, s32[2048]{0:T(1024)S(1)} %pad_clamp_fusion), kind=kCustom, calls=%fused_computation.8.clone | custom fusion | bytes 23808 | tf_op jit(solution)/shard_map/jit(_take)/gather | solution.py:345
  380.9 2.9 gather_fusion.13
  385.5 66.0 %psum.59 = f32[]{:T(128)} all-reduce(f32[]{:T(128)} %multiply_reduce_fusion.4), channel_id=1, replica_groups=mesh['gx'=8,'gy'=16] {'gx','gy'}, use_global_device_ids=true, to_apply=%region_15.20 | all-reduce | flops 1 | bytes 8 | tf_op jit(solution)/shard_map/psum | solution.py:202
  453.5 64.1 %psum.60 = f32[]{:T(128)} all-reduce(f32[]{:T(128)} %get-tuple-element.21), channel_id=1, replica_groups=mesh['gx'=8,'gy'=16] {'gx','gy'}, use_global_device_ids=true, to_apply=%region_17.22 | all-reduce | flops 1 | bytes 8 | tf_op jit(solution)/shard_map/psum | solution.py:198
  519.9 1.3 collective-permute-start.26
  521.2 1.3 collective-permute-start.25
  522.5 1.3 collective-permute-start.27
  523.8 4.0 collective-permute-start.24
  527.8 6.1 collective-permute-start.23
  533.9 4.9 collective-permute-start.22
  540.2 3.4 collective-permute-start.29
  544.8 11.5 %gather_fusion.15 = f32[1984]{0:T(1024)S(1)} fusion(f32[43008]{0:T(1024)S(1)} %bitcast.202, s32[2048]{0:T(1024)S(1)} %pad_clamp_fusion), kind=kCustom, calls=%fused_computation.9.clone | custom fusion | bytes 23808 | tf_op jit(solution)/shard_map/jit(_take)/gather | solution.py:345
  556.7 2.9 gather_fusion.16
  561.3 66.2 %psum.61 = f32[]{:T(128)} all-reduce(f32[]{:T(128)} %multiply_reduce_fusion.2), channel_id=1, replica_groups=mesh['gx'=8,'gy'=16] {'gx','gy'}, use_global_device_ids=true, to_apply=%region_19.24 | all-reduce | flops 1 | bytes 8 | tf_op jit(solution)/shard_map/psum | solution.py:202
  629.6 64.2 %psum.62 = f32[]{:T(128)} all-reduce(f32[]{:T(128)} %multiply_reduce_fusion.1), channel_id=1, replica_groups=mesh['gx'=8,'gy'=16] {'gx','gy'}, use_global_device_ids=true, to_apply=%region_21.26 | all-reduce | flops 1 | bytes 8 | tf_op jit(solution)/shard_map/psum | solution.py:198
  696.2 1.3 collective-permute-start.34
  700.1 4.0 collective-permute-start.32
  704.1 6.1 collective-permute-start.31
  710.2 4.9 collective-permute-start.30
  716.5 3.4 collective-permute-start.37
  721.2 11.5 %gather_fusion.18 = f32[1984]{0:T(1024)S(1)} fusion(f32[43008]{0:T(1024)S(1)} %bitcast.199, s32[2048]{0:T(1024)S(1)} %pad_clamp_fusion), kind=kCustom, calls=%fused_computation.10.clone | custom fusion | bytes 23808 | tf_op jit(solution)/shard_map/jit(_take)/gather | solution.py:345
  733.1 2.9 gather_fusion.19
  737.7 66.0 %psum.63 = f32[]{:T(128)} all-reduce(f32[]{:T(128)} %multiply_reduce_fusion), channel_id=1, replica_groups=mesh['gx'=8,'gy'=16] {'gx','gy'}, use_global_device_ids=true, to_apply=%region_23.28 | all-reduce | flops 1 | bytes 8 | tf_op jit(solution)/shard_map/psum | solution.py:202
  805.7 2.8 collective-permute-start.39
  809.9 3.1 collective-permute-done.38
  (416 shorter events, 58.9 us)
Async XLA Ops:
  3.1 25.8 %copy-start.51 = (s32[124]{0:T(128)S(1)}, s32[124]{0:T(128)}, u32[]{:S(2)}) copy-start(s32[124]{0:T(128)} %constant.341.clone) | copy-start | bytes 1492
  3.1 25.8 %copy-start.53 = (s32[124]{0:T(128)S(1)}, s32[124]{0:T(128)}, u32[]{:S(2)}) copy-start(s32[124]{0:T(128)} %constant.340.clone) | copy-start | bytes 1492
  3.1 26.6 %copy-start.41 = (f32[16]{0:T(128)S(1)}, f32[16]{0:T(128)}, u32[]{:S(2)}) copy-start(f32[16]{0:T(128)} %param.19) | copy-start | bytes 196
  4.3 48.6 %copy-start.55 = (s32[988]{0:T(1024)S(1)}, s32[988]{0:T(1024)}, u32[]{:S(2)}) copy-start(s32[988]{0:T(1024)} %constant.429) | copy-start | bytes 11860
  4.3 48.6 %copy-start.59 = (s32[116]{0:T(128)S(1)}, s32[116]{0:T(128)}, u32[]{:S(2)}) copy-start(s32[116]{0:T(128)} %constant.428) | copy-start | bytes 1396
  4.3 49.9 %copy-start.42 = (f32[48,288]{1,0:T(8,128)S(1)}, f32[48,288]{1,0:T(8,128)}, u32[]{:S(2)}) copy-start(f32[48,288]{1,0:T(8,128)} %param.20) | copy-start | bytes 165892
  4.3 63.9 %collective-permute-start.1 = (f32[4,16,48,1]{2,1,3,0:T(8,128)}, f32[4,16,48,1]{2,1,3,0:T(8,128)}, u32[]{:S(2)}, u32[]{:S(2)}) collective-permute-start(f32[4,16,48,1]{2,1,3,0:T(8,128)} %copy.274), channel_id=1, source_target_pairs={{16,0},{32,16},{48,32},{64,48},{80,64},{96,80},{112,96},{0,112},{1... | collective-permute-start | bytes 36872 | tf_op jit(solution)/shard_map/ppermute | solution.py:25
  6.3 61.3 %collective-permute-start = (f32[4,16,48,1]{2,1,3,0:T(8,128)S(1)}, f32[4,16,48,1]{2,1,3,0:T(8,128)S(1)}, u32[]{:S(2)}, u32[]{:S(2)}) collective-permute-start(f32[4,16,48,1]{2,1,3,0:T(8,128)S(1)} %copy.273), channel_id=1, source_target_pairs={{0,16},{16,32},{32,48},{48,64},{64,80},{80,96},{96,112},{112,0},{1... | collective-permute-start | bytes 36872 | tf_op jit(solution)/shard_map/ppermute | solution.py:24
  28.3 25.3 %copy-start.47 = (s32[16]{0:T(128)}, s32[16]{0:T(128)S(1)}, u32[]{:S(2)}) copy-start(s32[16]{0:T(128)S(1)} %get-tuple-element.29) | copy-start | bytes 196
  28.8 24.7 %copy-start.49 = (s32[16]{0:T(128)}, s32[16]{0:T(128)S(1)}, u32[]{:S(2)}) copy-start(s32[16]{0:T(128)S(1)} %fusion.115) | copy-start | bytes 196
  54.2 12.4 %copy-start.43 = (f32[48,288]{1,0:T(8,128)S(1)}, f32[48,288]{1,0:T(8,128)}, u32[]{:S(2)}) copy-start(f32[48,288]{1,0:T(8,128)} %param.21) | copy-start | bytes 165892
  68.2 12.8 %slice-start = ((s8[4718592]{0:T(1024)(128)(4,1)}), s8[524288]{0:T(1024)(128)(4,1)S(1)}, s32[]{:S(2)}) async-start(s8[4718592]{0:T(1024)(128)(4,1)} %bitcast.203), calls=%async_computation | async-start | bytes 1048576
  70.7 10.3 %slice-start.1 = ((s8[4718592]{0:T(1024)(128)(4,1)}), s8[4194304]{0:T(1024)(128)(4,1)S(1)}, s32[]{:S(2)}) async-start(s8[4718592]{0:T(1024)(128)(4,1)} %bitcast.203), calls=%async_computation.1 | async-start | bytes 8388608
  70.7 10.3 %copy-start.1 = (f32[4,16,48,1]{3,2,1,0:T(8,128)S(1)}, f32[4,16,48,1]{3,2,1,0:T(8,128)}, u32[]{:S(2)}) copy-start(f32[4,16,48,1]{3,2,1,0:T(8,128)} %copy.212) | copy-start | bytes 36868
  73.0 7.7 collective-permute-start.3
  74.5 6.4 collective-permute-start.2
  102.4 9.9 %copy-start.2 = (f32[2,16,48,288]{3,2,1,0:T(8,128)}, f32[2,16,48,288]{3,2,1,0:T(8,128)S(1)}, u32[]{:S(2)}) copy-start(f32[2,16,48,288]{3,2,1,0:T(8,128)S(1)} %constant_dynamic-update-slice_fusion) | copy-start | bytes 5308420
  102.4 12.3 %copy-start.4 = (s32[16,2,8,8]{3,2,1,0:T(8,128)S(1)}, s32[16,2,8,8]{3,2,1,0:T(8,128)}, u32[]{:S(2)}) copy-start(s32[16,2,8,8]{3,2,1,0:T(8,128)} %get-tuple-element.118) | copy-start | bytes 24580
  102.4 12.4 %copy-start.3 = (s32[16,2,8,8]{3,2,1,0:T(8,128)S(1)}, s32[16,2,8,8]{3,2,1,0:T(8,128)}, u32[]{:S(2)}) copy-start(s32[16,2,8,8]{3,2,1,0:T(8,128)} %get-tuple-element.119) | copy-start | bytes 24580
  104.0 6.1 collective-permute-start.5
  105.9 5.0 collective-permute-start.4
  113.3 62.0 %collective-permute-start.10 = (f32[16,128]{0,1:T(8,128)S(1)}, f32[16,128]{0,1:T(8,128)S(1)}, u32[]{:S(2)}, u32[]{:S(2)}) collective-permute-start(f32[16,128]{0,1:T(8,128)S(1)} %get-tuple-element.130), channel_id=1, source_target_pairs={{2,0},{3,1},{4,2},{5,3},{6,4},{7,5},{8,6},{9,7},{10,8},{11,9},{12,... | collective-permute-start | bytes 24584 | tf_op jit(solution)/shard_map/ppermute | solution.py:33
  126.4 11.7 %copy-start = (s32[864]{0:T(1024)S(1)}, s32[864]{0:T(1024)}, u32[]{:S(2)}) copy-start(s32[864]{0:T(1024)} %constant.338.clone) | copy-start | bytes 10372
  126.4 11.7 %copy-start.46 = (s32[2048]{0:T(1024)S(1)}, s32[2048]{0:T(1024)}, u32[]{:S(2)}) copy-start(s32[2048]{0:T(1024)} %get-tuple-element.158) | copy-start | bytes 24580
  146.6 35.9 %copy-start.48 = (s32[16]{0:T(128)S(1)}, s32[16]{0:T(128)}, u32[]{:S(2)}) copy-start(s32[16]{0:T(128)} %copy-done.47) | copy-start | bytes 196
  146.6 35.9 %copy-start.50 = (s32[16]{0:T(128)S(1)}, s32[16]{0:T(128)}, u32[]{:S(2)}) copy-start(s32[16]{0:T(128)} %copy-done.49) | copy-start | bytes 196
  146.6 35.9 %copy-start.52 = (s32[124]{0:T(128)S(1)}, s32[124]{0:T(128)}, u32[]{:S(2)}) copy-start(s32[124]{0:T(128)} %constant.341.clone) | copy-start | bytes 1492
  146.6 35.9 %copy-start.54 = (s32[124]{0:T(128)S(1)}, s32[124]{0:T(128)}, u32[]{:S(2)}) copy-start(s32[124]{0:T(128)} %constant.340.clone) | copy-start | bytes 1492
  158.2 24.6 %collective-permute-start.9 = (f32[16,128]{0,1:T(8,128)S(1)}, f32[16,128]{0,1:T(8,128)S(1)}, u32[]{:S(2)}, u32[]{:S(2)}) collective-permute-start(f32[16,128]{0,1:T(8,128)S(1)} %get-tuple-element.130), channel_id=1, source_target_pairs={{1,0},{2,1},{3,2},{4,3},{5,4},{6,5},{7,6},{8,7},{9,8},{10,9},{11,1... | collective-permute-start | bytes 24584 | tf_op jit(solution)/shard_map/ppermute | solution.py:33
  159.5 23.4 %collective-permute-start.11 = (f32[16,128]{0,1:T(8,128)S(1)}, f32[16,128]{0,1:T(8,128)S(1)}, u32[]{:S(2)}, u32[]{:S(2)}) collective-permute-start(f32[16,128]{0,1:T(8,128)S(1)} %get-tuple-element.130), channel_id=1, source_target_pairs={{3,0},{4,1},{5,2},{6,3},{7,4},{8,5},{9,6},{10,7},{11,8},{12,9},{13... | collective-permute-start | bytes 24584 | tf_op jit(solution)/shard_map/ppermute | solution.py:33
  160.8 22.2 %collective-permute-start.8 = (f32[16,128]{0,1:T(8,128)S(1)}, f32[16,128]{0,1:T(8,128)S(1)}, u32[]{:S(2)}, u32[]{:S(2)}) collective-permute-start(f32[16,128]{0,1:T(8,128)S(1)} %get-tuple-element.130), channel_id=1, source_target_pairs={{0,1},{1,2},{2,3},{3,4},{4,5},{5,6},{6,7},{7,8},{8,9},{9,10},{10,1... | collective-permute-start | bytes 24584 | tf_op jit(solution)/shard_map/ppermute | solution.py:33
  165.2 17.9 %collective-permute-start.7 = (f32[16,128]{0,1:T(8,128)S(1)}, f32[16,128]{0,1:T(8,128)S(1)}, u32[]{:S(2)}, u32[]{:S(2)}) collective-permute-start(f32[16,128]{0,1:T(8,128)S(1)} %get-tuple-element.130), channel_id=1, source_target_pairs={{0,2},{1,3},{2,4},{3,5},{4,6},{5,7},{6,8},{7,9},{8,10},{9,11},{10,... | collective-permute-start | bytes 24584 | tf_op jit(solution)/shard_map/ppermute | solution.py:33
  175.3 8.8 %collective-permute-start.6 = (f32[16,128]{0,1:T(8,128)S(1)}, f32[16,128]{0,1:T(8,128)S(1)}, u32[]{:S(2)}, u32[]{:S(2)}) collective-permute-start(f32[16,128]{0,1:T(8,128)S(1)} %get-tuple-element.130), channel_id=1, source_target_pairs={{0,3},{1,4},{2,5},{3,6},{4,7},{5,8},{6,9},{7,10},{8,11},{9,12},{10... | collective-permute-start | bytes 24584 | tf_op jit(solution)/shard_map/ppermute | solution.py:33
  184.2 6.8 collective-permute-start.13
  188.8 2.2 collective-permute-start.12
  344.0 14.0 %collective-permute-start.18 = (f32[16,128]{0,1:T(8,128)S(1)}, f32[16,128]{0,1:T(8,128)S(1)}, u32[]{:S(2)}, u32[]{:S(2)}) collective-permute-start(f32[16,128]{0,1:T(8,128)S(1)} %get-tuple-element.128), channel_id=1, source_target_pairs={{2,0},{3,1},{4,2},{5,3},{6,4},{7,5},{8,6},{9,7},{10,8},{11,9},{12,... | collective-permute-start | bytes 24584 | tf_op jit(solution)/shard_map/ppermute | solution.py:33
  345.3 17.7 %collective-permute-start.17 = (f32[16,128]{0,1:T(8,128)S(1)}, f32[16,128]{0,1:T(8,128)S(1)}, u32[]{:S(2)}, u32[]{:S(2)}) collective-permute-start(f32[16,128]{0,1:T(8,128)S(1)} %get-tuple-element.128), channel_id=1, source_target_pairs={{1,0},{2,1},{3,2},{4,3},{5,4},{6,5},{7,6},{8,7},{9,8},{10,9},{11,1... | collective-permute-start | bytes 24584 | tf_op jit(solution)/shard_map/ppermute | solution.py:33
  346.6 16.5 %collective-permute-start.19 = (f32[16,128]{0,1:T(8,128)S(1)}, f32[16,128]{0,1:T(8,128)S(1)}, u32[]{:S(2)}, u32[]{:S(2)}) collective-permute-start(f32[16,128]{0,1:T(8,128)S(1)} %get-tuple-element.128), channel_id=1, source_target_pairs={{3,0},{4,1},{5,2},{6,3},{7,4},{8,5},{9,6},{10,7},{11,8},{12,9},{13... | collective-permute-start | bytes 24584 | tf_op jit(solution)/shard_map/ppermute | solution.py:33
  347.9 15.3 %collective-permute-start.16 = (f32[16,128]{0,1:T(8,128)S(1)}, f32[16,128]{0,1:T(8,128)S(1)}, u32[]{:S(2)}, u32[]{:S(2)}) collective-permute-start(f32[16,128]{0,1:T(8,128)S(1)} %get-tuple-element.128), channel_id=1, source_target_pairs={{0,1},{1,2},{2,3},{3,4},{4,5},{5,6},{6,7},{7,8},{8,9},{9,10},{10,1... | collective-permute-start | bytes 24584 | tf_op jit(solution)/shard_map/ppermute | solution.py:33
  351.9 11.4 %collective-permute-start.15 = (f32[16,128]{0,1:T(8,128)S(1)}, f32[16,128]{0,1:T(8,128)S(1)}, u32[]{:S(2)}, u32[]{:S(2)}) collective-permute-start(f32[16,128]{0,1:T(8,128)S(1)} %get-tuple-element.128), channel_id=1, source_target_pairs={{0,2},{1,3},{2,4},{3,5},{4,6},{5,7},{6,8},{7,9},{8,10},{9,11},{10,... | collective-permute-start | bytes 24584 | tf_op jit(solution)/shard_map/ppermute | solution.py:33
  358.1 6.2 collective-permute-start.14
  364.4 4.3 collective-permute-start.21
  367.8 1.3 collective-permute-start.20
  519.9 14.0 %collective-permute-start.26 = (f32[16,128]{0,1:T(8,128)S(1)}, f32[16,128]{0,1:T(8,128)S(1)}, u32[]{:S(2)}, u32[]{:S(2)}) collective-permute-start(f32[16,128]{0,1:T(8,128)S(1)} %get-tuple-element.126), channel_id=1, source_target_pairs={{2,0},{3,1},{4,2},{5,3},{6,4},{7,5},{8,6},{9,7},{10,8},{11,9},{12,... | collective-permute-start | bytes 24584 | tf_op jit(solution)/shard_map/ppermute | solution.py:33
  521.2 17.7 %collective-permute-start.25 = (f32[16,128]{0,1:T(8,128)S(1)}, f32[16,128]{0,1:T(8,128)S(1)}, u32[]{:S(2)}, u32[]{:S(2)}) collective-permute-start(f32[16,128]{0,1:T(8,128)S(1)} %get-tuple-element.126), channel_id=1, source_target_pairs={{1,0},{2,1},{3,2},{4,3},{5,4},{6,5},{7,6},{8,7},{9,8},{10,9},{11,1... | collective-permute-start | bytes 24584 | tf_op jit(solution)/shard_map/ppermute | solution.py:33
  522.5 16.5 %collective-permute-start.27 = (f32[16,128]{0,1:T(8,128)S(1)}, f32[16,128]{0,1:T(8,128)S(1)}, u32[]{:S(2)}, u32[]{:S(2)}) collective-permute-start(f32[16,128]{0,1:T(8,128)S(1)} %get-tuple-element.126), channel_id=1, source_target_pairs={{3,0},{4,1},{5,2},{6,3},{7,4},{8,5},{9,6},{10,7},{11,8},{12,9},{13... | collective-permute-start | bytes 24584 | tf_op jit(solution)/shard_map/ppermute | solution.py:33
  523.8 15.3 %collective-permute-start.24 = (f32[16,128]{0,1:T(8,128)S(1)}, f32[16,128]{0,1:T(8,128)S(1)}, u32[]{:S(2)}, u32[]{:S(2)}) collective-permute-start(f32[16,128]{0,1:T(8,128)S(1)} %get-tuple-element.126), channel_id=1, source_target_pairs={{0,1},{1,2},{2,3},{3,4},{4,5},{5,6},{6,7},{7,8},{8,9},{9,10},{10,1... | collective-permute-start | bytes 24584 | tf_op jit(solution)/shard_map/ppermute | solution.py:33
  527.8 11.4 %collective-permute-start.23 = (f32[16,128]{0,1:T(8,128)S(1)}, f32[16,128]{0,1:T(8,128)S(1)}, u32[]{:S(2)}, u32[]{:S(2)}) collective-permute-start(f32[16,128]{0,1:T(8,128)S(1)} %get-tuple-element.126), channel_id=1, source_target_pairs={{0,2},{1,3},{2,4},{3,5},{4,6},{5,7},{6,8},{7,9},{8,10},{9,11},{10,... | collective-permute-start | bytes 24584 | tf_op jit(solution)/shard_map/ppermute | solution.py:33
  533.9 6.2 collective-permute-start.22
  540.2 4.3 collective-permute-start.29
  543.6 1.3 collective-permute-start.28
  556.5 73.0 %copy-start.61 = (s32[16]{0:T(128)S(1)}, s32[16]{0:T(128)}, u32[]{:S(2)}) copy-start(s32[16]{0:T(128)} %get-tuple-element.18) | copy-start | bytes 196
  559.6 155.5 %copy-start.60 = (s32[1,1,16]{2,1,0:T(1,128)S(1)}, s32[1,1,16]{2,1,0:T(1,128)}, u32[]{:S(2)}) copy-start(s32[1,1,16]{2,1,0:T(1,128)} %get-tuple-element.19) | copy-start | bytes 196
  696.2 14.0 %collective-permute-start.34 = (f32[16,128]{0,1:T(8,128)S(1)}, f32[16,128]{0,1:T(8,128)S(1)}, u32[]{:S(2)}, u32[]{:S(2)}) collective-permute-start(f32[16,128]{0,1:T(8,128)S(1)} %get-tuple-element.124), channel_id=1, source_target_pairs={{2,0},{3,1},{4,2},{5,3},{6,4},{7,5},{8,6},{9,7},{10,8},{11,9},{12,... | collective-permute-start | bytes 24584 | tf_op jit(solution)/shard_map/ppermute | solution.py:33
  697.5 17.8 %collective-permute-start.33 = (f32[16,128]{0,1:T(8,128)S(1)}, f32[16,128]{0,1:T(8,128)S(1)}, u32[]{:S(2)}, u32[]{:S(2)}) collective-permute-start(f32[16,128]{0,1:T(8,128)S(1)} %get-tuple-element.124), channel_id=1, source_target_pairs={{1,0},{2,1},{3,2},{4,3},{5,4},{6,5},{7,6},{8,7},{9,8},{10,9},{11,1... | collective-permute-start | bytes 24584 | tf_op jit(solution)/shard_map/ppermute | solution.py:33
  698.8 16.5 %collective-permute-start.35 = (f32[16,128]{0,1:T(8,128)S(1)}, f32[16,128]{0,1:T(8,128)S(1)}, u32[]{:S(2)}, u32[]{:S(2)}) collective-permute-start(f32[16,128]{0,1:T(8,128)S(1)} %get-tuple-element.124), channel_id=1, source_target_pairs={{3,0},{4,1},{5,2},{6,3},{7,4},{8,5},{9,6},{10,7},{11,8},{12,9},{13... | collective-permute-start | bytes 24584 | tf_op jit(solution)/shard_map/ppermute | solution.py:33
  700.1 15.3 %collective-permute-start.32 = (f32[16,128]{0,1:T(8,128)S(1)}, f32[16,128]{0,1:T(8,128)S(1)}, u32[]{:S(2)}, u32[]{:S(2)}) collective-permute-start(f32[16,128]{0,1:T(8,128)S(1)} %get-tuple-element.124), channel_id=1, source_target_pairs={{0,1},{1,2},{2,3},{3,4},{4,5},{5,6},{6,7},{7,8},{8,9},{9,10},{10,1... | collective-permute-start | bytes 24584 | tf_op jit(solution)/shard_map/ppermute | solution.py:33
  704.1 11.4 %collective-permute-start.31 = (f32[16,128]{0,1:T(8,128)S(1)}, f32[16,128]{0,1:T(8,128)S(1)}, u32[]{:S(2)}, u32[]{:S(2)}) collective-permute-start(f32[16,128]{0,1:T(8,128)S(1)} %get-tuple-element.124), channel_id=1, source_target_pairs={{0,2},{1,3},{2,4},{3,5},{4,6},{5,7},{6,8},{7,9},{8,10},{9,11},{10,... | collective-permute-start | bytes 24584 | tf_op jit(solution)/shard_map/ppermute | solution.py:33
  710.2 6.2 collective-permute-start.30
  716.5 4.3 collective-permute-start.37
  719.9 1.3 collective-permute-start.36
  732.9 72.8 %copy-start.57 = (pred[2]{0:T(512)(128)(4,1)S(1)}, pred[2]{0:T(512)(128)(4,1)}, u32[]{:S(2)}) copy-start(pred[2]{0:T(512)(128)(4,1)} %get-tuple-element.154) | copy-start | bytes 10
  805.7 4.2 collective-permute-start.39
  808.6 4.4 collective-permute-start.38
  (40 other events, 207.9 us)
where the time goes:
time: 819 us; the launch traced here: 815 us
  blocking collectives  459 us (56%)
  local copies, waits for them, and re-layouts  129 us (16%)
  starting transfers between devices  115 us (14%)
  other arithmetic  61.4 us (7%)
  between operations  37.3 us (5%)
  waiting for transfers between devices  13 us (2%)
    psum x4, blocking collectives, norm_sum(): return lax.psum(jnp.sum(first_field * second_field), ('gx', 'gy'))  261 us
    psum x3, blocking collectives, curvature_sum(): return lax.psum(jnp.sum(first_field * second_field), ('gx', 'gy'))  198 us
    ppermute x24, starting transfers between devices, shifted(): lax.ppermute(value, axis, [(source, source + steps) for source in range(f...  82.1 us
    gather x8, local copies, waits for them, and re-layouts, apply_curve(): cycle_values = jnp.take(shared.reshape(-1), cycle_source) * usable_float  46.2 us
    ppermute x8, starting transfers between devices, extended_2(): after = lax.ppermute(first, axis, down)  20.1 us
  transfers between devices with their start and end apart: 40, of which 13 were waited for; matrix products, arithmetic and copies ran while one was open for 10% of the time, Pallas kernels for 0%

commit v1 on v0

v1 whole, which is shorter than its diff:
```python
import functools

import jax
import jax.numpy as jnp
from jax import lax
from jax.experimental import pallas as pl
from jax.experimental.pallas import tpu as pltpu
from jax.sharding import PartitionSpec as P

BLAT = 24
BLON = 36
LEV = 16
ROWS = 48
COLS = 288
WIDE = 384
EXT = 56
TILES = ROWS // 8

f32 = jnp.float32
MESH = pl.DeviceIdType.MESH

NORTH, SOUTH, EAST, WEST = (0, 1), (0, -1), (1, 0), (-1, 0)
DIAGONAL = ((1, 1), (-1, 1), (1, -1), (-1, -1))


def iota(shape, dim):
    return lax.broadcasted_iota(jnp.int32, shape, dim)


def padded(value):
    return jnp.concatenate([value, jnp.zeros((value.shape[0], WIDE - COLS), f32)], axis=1)


def east_of(value):
    return pltpu.roll(value, WIDE - 1, 1)


def west_of(value):
    return pltpu.roll(value, 1, 1)


def inverse(value):
    guess = pl.reciprocal(value, approx=True)
    return guess * (2.0 - value * guess)


def row_pack(low, high):
    return jnp.where(iota(low.shape, 0) < 4, low, high)


def column_pack(first, last):
    lane = iota(first.shape, 1)
    low = pltpu.roll(first, 32, 1)
    high = pltpu.roll(last, 96, 1)
    return jnp.where(
        (lane >= 32) & (lane < 36), low, jnp.where(lane >= 124, high, 0.0)
    )


def kernel(
    nx,
    ny,
    ocean,
    thick,
    mixing,
    damping,
    blocks,
    tracer_out,
    surface_out,
    state,
    h,
    mix,
    damp,
    blk,
    mask,
    level_inv,
    flat,
    send_rows,
    send_heat,
    recv_rows,
    recv_heat,
    send_cols,
    recv_cols,
    send_corner,
    recv_corner,
    flux_lon,
    flux_north,
    flux_prev,
    ratio,
    scale,
    basis,
    halo_rows,
    halo_cols,
    halo_corner,
    recv_halo_rows,
    recv_halo_cols,
    recv_halo_corner,
    message,
    first_sum,
    second_message,
    second_sum,
    load_sem,
    small_sem,
    send_sem,
    recv_sem,
    halo_send_sem,
    halo_recv_sem,
    sum_send_sem,
    sum_recv_sem,
):
    gx = lax.axis_index("gx")
    gy = lax.axis_index("gy")

    def device(step):
        return {"gx": lax.rem(gx + step[0] + nx, nx), "gy": lax.rem(gy + step[1] + ny, ny)}

    partners = []
    for step in (
        [NORTH, SOUTH, EAST, WEST, *DIAGONAL]
        + [(d, 0) for d in range(1, nx)]
        + [(0, d) for d in range(1, ny)]
    ):
        step = (step[0] % nx, step[1] % ny)
        if step != (0, 0) and step not in partners:
            partners.append(step)

    barrier = pltpu.get_barrier_semaphore()
    for step in partners:
        pl.semaphore_signal(barrier, inc=1, device_id=device(step), device_id_type=MESH)

    small = [
        pltpu.make_async_copy(blocks, blk, small_sem.at[0]),
        pltpu.make_async_copy(thick, h, small_sem.at[1]),
        pltpu.make_async_copy(damping, damp, small_sem.at[2]),
        pltpu.make_async_copy(mixing, mix, small_sem.at[3]),
    ]
    loads = []
    for index, (start, size) in enumerate(((0, 8), (40, 8), (8, 16), (24, 16))):
        rows = pl.ds(start, size)
        loads.append(
            pltpu.make_async_copy(
                ocean.at[:, :, rows, :], state.at[:, :, rows, :], load_sem.at[index]
            )
        )
    for copy in small[:3] + loads + small[3:]:
        copy.start()

    block_rows, block_cols = blk.shape
    small[0].wait()
    row = iota((EXT, block_rows), 0)
    row = gy * ROWS + jnp.where(row < ROWS + 4, row, row - EXT)
    edge = iota((EXT, block_rows), 1) * BLAT
    pick_rows = jnp.where((row >= edge) & (row < edge + BLAT), 1.0, 0.0)
    lane = iota((block_cols, WIDE), 1)
    total = block_cols * BLON
    col = gx * COLS + jnp.where(lane < COLS + 4, lane, lane - WIDE)
    col = jnp.where(col < 0, col + total, jnp.where(col >= total, col - total, col))
    edge = iota((block_cols, WIDE), 0) * BLON
    inside = (lane < COLS + 4) | (lane >= WIDE - 4)
    pick_cols = jnp.where(inside & (col >= edge) & (col < edge + BLON), 1.0, 0.0)
    coarse = jnp.dot(pick_rows, blk[...].astype(f32), preferred_element_type=f32)
    mask[...] = jnp.dot(coarse, pick_cols, preferred_element_type=f32)

    small[1].wait()
    level_inv[...] = jnp.zeros(level_inv.shape, f32)
    for k in range(1, LEV):
        level_inv[k : k + 1, :] = 1.0 / jnp.full((1, WIDE), h[k - 1] + h[k], f32)

    small[2].wait()
    damp_low = padded(damp[0:8, :])
    damp_high = padded(damp[ROWS - 8 : ROWS, :])
    damp_rows = row_pack(damp_low, damp_high)
    for side in range(2):
        send_rows[side, 32:40, :] = damp_rows
    damp_all = padded(damp[...])
    send_cols[ROWS:, :] = column_pack(damp_all[:, 0:128], damp_all[:, 256:384])
    send_corner[...] = column_pack(damp_rows[:, 0:128], damp_rows[:, 256:384])

    def remote(source, target, index, step, sends=send_sem, recvs=recv_sem):
        return pltpu.make_async_remote_copy(
            src_ref=source,
            dst_ref=target,
            send_sem=sends.at[index],
            recv_sem=recvs.at[index],
            device_id=device(step),
            device_id_type=MESH,
        )

    loads[0].wait()
    loads[1].wait()
    pl.semaphore_wait(barrier, len(partners))
    first_round = []
    for side, (edge_row, step) in enumerate(((ROWS - 1, NORTH), (0, SOUTH))):
        edge_mask = mask[edge_row : edge_row + 1, :]
        heat = padded(state[0, :, edge_row, :]) * edge_mask
        salt = padded(state[1, :, edge_row, :]) * edge_mask
        send_heat[side] = heat
        send_rows[side, 0:16, :] = heat - 0.5 * salt
        send_rows[side, 16:32, :] = padded(state[3, :, edge_row, :]) * edge_mask
        copy = remote(send_rows.at[side], recv_rows.at[side], side, step)
        copy.start()
        first_round.append(copy)

    lane128 = iota((8, 128), 1)

    def pack_columns(i, _):
        rows = pl.ds(pl.multiple_of(8 * i, 8), 8)
        edge_mask = jnp.where(lane128 == 31, mask[rows, 256:384], mask[rows, 0:128])
        acc_west = jnp.zeros((8, 128), f32)
        acc_east = jnp.zeros((8, 128), f32)
        for field, base in ((0, 0), (1, 16), (2, 64)):
            for k in range(LEV):
                first = state[field, k, rows, 0:128]
                last = jnp.concatenate(
                    [state[field, k, rows, 256:COLS], jnp.zeros((8, WIDE - COLS), f32)], axis=1
                )
                merged = jnp.where(lane128 == 31, last, first)
                turned = pltpu.roll(merged, base + k, 1) if base + k else merged
                acc_west = jnp.where(lane128 == base + k, turned, acc_west)
                acc_east = jnp.where(lane128 == base + k + 31, turned, acc_east)
        west_mask = jnp.broadcast_to(edge_mask[:, 0:1], (8, 128))
        east_mask = jnp.broadcast_to(edge_mask[:, 31:32], (8, 128))
        send_cols[rows, :] = acc_west * west_mask + pltpu.roll(acc_east, 1, 1) * east_mask
        return 0

    pack_columns(0, 0)
    pack_columns(5, 0)
    loads[2].wait()
    lax.fori_loop(1, 3, pack_columns, 0)
    loads[3].wait()
    lax.fori_loop(3, 5, pack_columns, 0)
    for side, step in enumerate((EAST, WEST)):
        copy = remote(send_cols, recv_cols.at[side], 2 + side, step)
        copy.start()
        first_round.append(copy)
    for place, step in enumerate(DIAGONAL):
        copy = remote(send_corner, recv_corner.at[place], 4 + place, step)
        copy.start()
        first_round.append(copy)
    heat_round = []
    for side, step in enumerate((NORTH, SOUTH)):
        copy = remote(send_heat.at[side], recv_heat.at[side], 8 + side, step)
        copy.start()
        heat_round.append(copy)

    sub = iota((8, WIDE), 0)

    def next_row(i):
        return jnp.minimum(8 * i + 8, ROWS - 1)

    def level_sums(i, _):
        rows = pl.ds(pl.multiple_of(8 * i, 8), 8)
        row = pl.ds(next_row(i), 1)
        here = mask[rows, :]
        beyond = mask[row, :]

        def level(k, carry):
            plain, lon, lat = carry
            s = padded(state[0, k, rows, :] - 0.5 * state[1, k, rows, :]) * here
            u = padded(state[2, k, rows, :]) * here
            v = padded(state[3, k, rows, :]) * here
            s_row = padded(state[0, k, row, :] - 0.5 * state[1, k, row, :]) * beyond
            v_row = padded(state[3, k, row, :]) * beyond
            s_north = jnp.where(sub == 7, s_row, pltpu.roll(s, 7, 0))
            v_north = jnp.where(sub == 7, v_row, pltpu.roll(v, 7, 0))
            weight = 0.05 * h[k]
            plain = plain + h[k] * s
            lon = lon + weight * (u + east_of(u)) * (s + east_of(s))
            lat = lat + weight * (v + v_north) * (s + s_north)
            return plain, lon, lat

        zero = jnp.zeros((8, WIDE), f32)
        plain, lon, lat = lax.fori_loop(0, LEV, level, (zero, zero, zero), unroll=4)
        flat[0, rows, :] = plain
        flat[1, rows, :] = lon
        flat[2, rows, :] = lat
        return 0

    lax.fori_loop(0, TILES, level_sums, 0)

    for copy in first_round:
        copy.wait()

    lane_c = iota((ROWS, 128), 1)
    own = send_cols[0:ROWS, :]
    is_east = (lane_c & 32) != 0
    other = jnp.where(
        is_east,
        pltpu.roll(recv_cols[1, 0:ROWS, :], 32, 1),
        pltpu.roll(recv_cols[0, 0:ROWS, :], 96, 1),
    )
    both = own + other
    speed = pltpu.roll(both, 64, 1)
    speed = jnp.where((lane_c & 16) != 0, pltpu.roll(speed, 16, 1), speed)
    slope = jnp.where(is_east, 0.1, -0.1) * (other - own)
    through = 0.05 * speed * both - slope
    flux_lon[...] = through
    weight = jnp.zeros((1, 128), f32)
    lane_w = iota((1, 128), 1)
    for k in range(LEV):
        weight = jnp.where((lane_w & 15) == k, h[k], weight)
    weight = weight * jnp.where((lane_w & 16) != 0, -0.5, 1.0)
    weighed = through * weight
    side_west = jnp.sum(jnp.where(lane_c < 32, weighed, 0.0), axis=1, keepdims=True)
    side_east = jnp.sum(
        jnp.where(is_east & (lane_c < 64), weighed, 0.0), axis=1, keepdims=True
    )

    level_weight = jnp.zeros((LEV, WIDE), f32)
    level_row = iota((LEV, WIDE), 0)
    for k in range(LEV):
        level_weight = jnp.where(level_row == k, h[k], level_weight)
    exists = (
        jnp.where(gy < ny - 1, 1.0, 0.0).astype(f32),
        jnp.where(gy > 0, 1.0, 0.0).astype(f32),
    )

    def side_flux(mine, theirs, speeds, sign):
        return speeds * (mine + theirs) - (0.1 * sign) * (theirs - mine)

    side_lat = []
    speed_lat = []
    for side, sign in ((0, 1.0), (1, -1.0)):
        slot = 1 - side
        s_mine = send_rows[side, 0:16, :]
        s_theirs = recv_rows[slot, 0:16, :] * exists[side]
        speeds = 0.05 * (send_rows[side, 16:32, :] + recv_rows[slot, 16:32, :] * exists[side])
        speed_lat.append(speeds)
        flux = side_flux(s_mine, s_theirs, speeds, sign)
        side_lat.append(jnp.sum(flux * level_weight, axis=0, keepdims=True))

    def assemble(center, rows_in, cols_in, corner_in):
        lane8 = iota((8, 128), 1)
        lane48 = iota((ROWS, 128), 1)
        third = jnp.where(
            lane48 < 32, center[:, 256:384], jnp.where(lane48 < 64, cols_in(1), cols_in(0))
        )
        upper = jnp.concatenate([center[:, 0:256], third], axis=1)
        north_south = jnp.where(sub < 4, rows_in(1), rows_in(0))
        north = jnp.where(lane8 < 64, corner_in(3), corner_in(2))
        south = jnp.where(lane8 < 64, corner_in(1), corner_in(0))
        corner = jnp.where(iota((8, 128), 0) < 4, north, south)
        third = jnp.where(lane8 < 32, north_south[:, 256:384], corner)
        lower = jnp.concatenate([north_south[:, 0:256], third], axis=1)
        return jnp.concatenate([upper, lower], axis=0)

    damp_ext = assemble(
        damp_all,
        lambda slot: recv_rows[slot, 32:40, :],
        lambda slot: recv_cols[slot, ROWS:, :],
        lambda place: recv_corner[place],
    )
    inv = mask[...] * inverse(6.0 + damp_ext)
    scale[...] = 1.5 * inv

    lane_f = iota((ROWS, WIDE), 1)
    row_f = iota((ROWS, WIDE), 0)
    plain = flat[0]
    lon = flat[1] - 0.1 * (east_of(plain) - plain)
    lon = jnp.where(lane_f == COLS - 1, side_east, jnp.where(lane_f == WIDE - 1, side_west, lon))
    lat = flat[2] - 0.1 * (pltpu.roll(plain, ROWS - 1, 0) - plain)
    lat = jnp.where(row_f == ROWS - 1, side_lat[0], lat)
    lat_south = jnp.where(row_f == 0, side_lat[1], pltpu.roll(lat, 1, 0))
    start = plain - (lon - west_of(lon)) - (lat - lat_south)
    start = jnp.where(lane_f < COLS, start, 0.0) * inv[0:ROWS, :]

    packed_rows = row_pack(start[0:8, :], start[ROWS - 8 : ROWS, :])
    halo_rows[...] = packed_rows
    halo_cols[...] = column_pack(start[:, 0:128], start[:, 256:384])
    halo_corner[...] = column_pack(packed_rows[:, 0:128], packed_rows[:, 256:384])
    second_round = []
    for side, step in enumerate((NORTH, SOUTH)):
        second_round.append(
            remote(halo_rows, recv_halo_rows.at[side], side, step, halo_send_sem, halo_recv_sem)
        )
    for side, step in enumerate((EAST, WEST)):
        second_round.append(
            remote(halo_cols, recv_halo_cols.at[side], 2 + side, step, halo_send_sem, halo_recv_sem)
        )
    for place, step in enumerate(DIAGONAL):
        second_round.append(
            remote(
                halo_corner,
                recv_halo_corner.at[place],
                4 + place,
                step,
                halo_send_sem,
                halo_recv_sem,
            )
        )
    for copy in second_round:
        copy.start()

    for copy in heat_round:
        copy.wait()
    for side, sign in ((0, 1.0), (1, -1.0)):
        slot = 1 - side
        target = flux_north if side == 0 else flux_prev
        heat_mine = send_heat[side]
        heat_theirs = recv_heat[slot] * exists[side]
        salt_mine = 2.0 * (heat_mine - send_rows[side, 0:16, :])
        salt_theirs = 2.0 * (heat_theirs - recv_rows[slot, 0:16, :] * exists[side])
        target[0:16, :] = side_flux(heat_mine, heat_theirs, speed_lat[side], sign)
        target[16:32, :] = side_flux(salt_mine, salt_theirs, speed_lat[side], sign)
    small[3].wait()

    edge_lane = (lane128 == 31) | (lane128 == 127)

    def mix_tile(i, _):
        rows = pl.ds(pl.multiple_of(8 * i, 8), 8)
        row = pl.ds(next_row(i), 1)
        here = mask[rows, :]
        beyond = mask[row, :]
        coefficient = padded(mix[rows, :])
        through = flux_lon[rows, :]
        use_north = (sub == 7) & (i == TILES - 1)

        def level(k, carry):
            ratio_low, heat_low, salt_low = carry
            u = padded(state[2, k, rows, :]) * here
            v = padded(state[3, k, rows, :]) * here
            v_row = padded(state[3, k, row, :]) * beyond
            v_north = jnp.where(sub == 7, v_row, pltpu.roll(v, 7, 0))
            u_pair = 0.05 * (u + east_of(u))
            v_pair = 0.05 * (v + v_north)
            lon_far, lon_near = u_pair - 0.1, u_pair + 0.1
            lat_far, lat_near = v_pair - 0.1, v_pair + 0.1
            below = coefficient * level_inv[pl.ds(k, 1), :]
            above = coefficient * level_inv[pl.ds(k + 1, 1), :]
            pivot = inverse(h[k] + above + below * (1.0 - ratio_low))
            ratio_now = above * pivot
            ratio[k] = ratio_now
            found = []
            for tracer, low in ((0, heat_low), (1, salt_low)):
                plane = tracer * LEV + k
                c = padded(state[tracer, k, rows, :]) * here
                c_row = padded(state[tracer, k, row, :]) * beyond
                c_north = jnp.where(sub == 7, c_row, pltpu.roll(c, 7, 0))
                lon = lon_far * east_of(c) + lon_near * c
                turned = pltpu.roll(through, 127 - plane, 1)
                lon = jnp.concatenate(
                    [lon[:, 0:256], jnp.where(edge_lane, turned, lon[:, 256:384])], axis=1
                )
                lat = lat_far * c_north + lat_near * c
                lat = jnp.where(use_north, flux_north[pl.ds(plane, 1), :], lat)
                lat_south = jnp.where(
                    sub == 0, flux_prev[pl.ds(plane, 1), :], pltpu.roll(lat, 1, 0)
                )
                flux_prev[pl.ds(plane, 1), :] = lat[7:8, :]
                advected = here * (c - (lon - west_of(lon)) - (lat - lat_south))
                value = (h[k] * advected + below * low) * pivot
                tracer_out[tracer, k, rows, :] = value[:, 0:COLS]
                found.append(value)
            return ratio_now, found[0], found[1]

        zero = jnp.zeros((8, WIDE), f32)
        _, heat, salt = lax.fori_loop(0, LEV, level, (zero, zero, zero), unroll=4)

        def back(step, carry):
            k = LEV - 2 - step
            heat_up, salt_up = carry
            share = ratio[k][:, 0:COLS]
            heat_up = tracer_out[0, k, rows, :] + share * heat_up
            salt_up = tracer_out[1, k, rows, :] + share * salt_up
            tracer_out[0, k, rows, :] = heat_up
            tracer_out[1, k, rows, :] = salt_up
            return heat_up, salt_up

        lax.fori_loop(0, LEV - 1, back, (heat[:, 0:COLS], salt[:, 0:COLS]), unroll=5)
        return 0

    lax.fori_loop(0, 2, mix_tile, 0)

    for copy in second_round:
        copy.wait()

    q = assemble(
        start,
        lambda slot: recv_halo_rows[slot],
        lambda slot: recv_halo_cols[slot],
        lambda place: recv_halo_corner[place],
    )
    q = q * mask[...]
    weight = jnp.where(lane_f < COLS, 6.0 + damp_all, 0.0)
    basis[0] = q
    previous = None
    message_rows = []
    for index in range(4):
        pair = east_of(q) + west_of(q)
        column = q + 0.5 * pair
        around = pair + pltpu.roll(column, EXT - 1, 0) + pltpu.roll(column, 1, 0)
        image = scale[...] * around - 0.5 * q
        after = image if previous is None else 2.0 * image - previous
        if index < 3:
            basis[index + 1] = after
        weighed = weight * q[0:ROWS, :]
        message_rows.append(weighed * q[0:ROWS, :])
        message_rows.append(weighed * after[0:ROWS, :])
        previous, q = q, after

    def folded(value):
        value = value[:, 0:128] + value[:, 128:256] + value[:, 256:384]
        return jnp.sum(value, axis=0, keepdims=True)

    message[...] = jnp.concatenate([folded(value) for value in message_rows], axis=0)

    def spread(source, target, count, axis, mine, base):
        target[mine] = source[...]
        copies = []
        for d in range(1, count):
            step = (d, 0) if axis == "gx" else (0, d)
            copies.append(
                pltpu.make_async_remote_copy(
                    src_ref=source,
                    dst_ref=target.at[mine],
                    send_sem=sum_send_sem.at[base],
                    recv_sem=sum_recv_sem.at[base],
                    device_id=device(step),
                    device_id_type=MESH,
                )
            )
        for copy in copies:
            copy.start()

    def gathered(target, count, base):
        part = target.at[pl.ds(0, count - 1)]
        done = pltpu.make_async_remote_copy(
            src_ref=part,
            dst_ref=part,
            send_sem=sum_send_sem.at[base],
            recv_sem=sum_recv_sem.at[base],
            device_id=device(EAST),
            device_id_type=MESH,
        )
        done.wait_recv()
        done.wait_send()
        return jnp.sum(target[...], axis=0)

    spread(message, first_sum, nx, "gx", gx, 0)
    lax.fori_loop(2, 4, mix_tile, 0)
    second_message[...] = gathered(first_sum, nx, 0)
    spread(second_message, second_sum, ny, "gy", gy, 1)
    lax.fori_loop(4, 6, mix_tile, 0)
    sums = gathered(second_sum, ny, 1)

    sums = jnp.broadcast_to(jnp.sum(sums, axis=1, keepdims=True), (8, 128))
    dots = [sums[i : i + 1, :] for i in range(8)]
    moment = dots[0:2] + [2.0 * dots[i] - dots[i % 2] for i in range(2, 8)]

    def gram(i, j):
        return 0.5 * (moment[i + j] + moment[abs(i - j)])

    lower = {}
    pivots = []
    right = []
    for i in range(4):
        value = moment[i]
        for j in range(i + 1):
            entry = gram(i, j) - 0.5 * (gram(j, i + 1) + gram(j, abs(i - 1)))
            for k in range(j):
                entry = entry - lower[i, k] * lower[j, k] * pivots[k]
            if j < i:
                lower[i, j] = entry / pivots[j]
                value = value - lower[i, j] * right[j]
            else:
                pivots.append(entry)
        right.append(value)
    solved = [None] * 4
    for i in range(3, -1, -1):
        value = right[i] / pivots[i]
        for j in range(i + 1, 4):
            value = value - lower[j, i] * solved[j]
        solved[i] = value
    surface = None
    for i in range(4):
        factor = 1.5 * solved[i]
        factor = jnp.concatenate([factor, factor, factor], axis=1)
        term = factor * basis[i, 0:ROWS, :]
        surface = term if surface is None else surface + term
    surface_out[...] = surface[:, 0:COLS]


def scratch(nx, ny):
    vmem = lambda *shape: pltpu.VMEM(shape, f32)
    dma = pltpu.SemaphoreType.DMA
    return [
        vmem(4, LEV, ROWS, COLS),
        pltpu.SMEM((LEV,), f32),
        vmem(ROWS, COLS),
        vmem(ROWS, COLS),
        None,
        vmem(EXT, WIDE),
        vmem(24, WIDE),
        vmem(3, ROWS, WIDE),
        vmem(2, 40, WIDE),
        vmem(2, LEV, WIDE),
        vmem(2, 40, WIDE),
        vmem(2, LEV, WIDE),
        vmem(2 * ROWS, 128),
        vmem(2, 2 * ROWS, 128),
        vmem(8, 128),
        vmem(4, 8, 128),
        vmem(ROWS, 128),
        vmem(2 * LEV, WIDE),
        vmem(2 * LEV, WIDE),
        vmem(LEV, 8, WIDE),
        vmem(EXT, WIDE),
        vmem(4, EXT, WIDE),
        vmem(8, WIDE),
        vmem(ROWS, 128),
        vmem(8, 128),
        vmem(2, 8, WIDE),
        vmem(2, ROWS, 128),
        vmem(4, 8, 128),
        vmem(8, 128),
        vmem(nx, 8, 128),
        vmem(8, 128),
        vmem(ny, 8, 128),
        dma((4,)),
        dma((4,)),
        dma((10,)),
        dma((10,)),
        dma((8,)),
        dma((8,)),
        dma((2,)),
        dma((2,)),
    ]


def solution(mesh):
    nx, ny = mesh.shape["gx"], mesh.shape["gy"]

    def body(ocean_state, layer_thickness, vertical_mixing, damping, ocean_blocks):
        shapes = scratch(nx, ny)
        shapes[4] = pltpu.VMEM(ocean_blocks.shape, jnp.int32)
        call = pl.pallas_call(
            functools.partial(kernel, nx, ny),
            out_shape=[
                pltpu.VMEM((2, LEV, ROWS, COLS), f32),
                pltpu.VMEM((ROWS, COLS), f32),
            ],
            in_specs=[pl.BlockSpec(memory_space=pltpu.HBM)] * 5,
            out_specs=[pl.BlockSpec(memory_space=pltpu.VMEM)] * 2,
            scratch_shapes=shapes,
            compiler_params=pltpu.CompilerParams(
                collective_id=0, has_side_effects=True, vmem_limit_bytes=32 * 1024 * 1024
            ),
        )
        operands = [
            pltpu.with_memory_space_constraint(operand, pltpu.HBM)
            for operand in (ocean_state, layer_thickness, vertical_mixing, damping, ocean_blocks)
        ]
        return tuple(call(*operands))

    def wrapped(*args):
        with jax.sharding.use_abstract_mesh(mesh.abstract_mesh):
            return jax.shard_map(
                body,
                mesh=mesh,
                in_specs=(P(None, None, "gy", "gx"), P(), P("gy", "gx"), P("gy", "gx"), P()),
                out_specs=(P(None, None, "gy", "gx"), P("gy", "gx")),
                check_vma=False,
            )(*args)

    return wrapped
```

time: 819 us -> 30.2 us (0.04)
  blocking collectives: 459 us -> 0 us
  local copies, waits for them, and re-layouts: 129 us -> 2.04 us
  starting transfers between devices: 115 us -> 0 us
  other arithmetic: 61.4 us -> 0 us
  between operations: 37.3 us -> 0.64 us
  Pallas kernels: 0 us -> 27.3 us
  waiting for transfers between devices: 13 us -> 0 us
    psum x7 -> x0, blocking collectives: 459 us -> none  [the longest x4 261 us: norm_sum(): return lax.psum(jnp.sum(first_field * second_field), ('gx', 'gy'))]
    ppermute x40 -> x0, starting transfers between devices: 115 us -> none  [the longest x24 82.1 us: shifted(): lax.ppermute(value, axis, [(source, source + steps) for source in range(f...]
    gather x33 -> x0, local copies, waits for them, and re-layouts: 107 us -> none  [the longest x8 46.2 us: apply_curve(): cycle_values = jnp.take(shared.reshape(-1), cycle_source) * usable_float]
    pallas_call x0 -> x1, Pallas kernels: none -> 27.3 us  [body(): return tuple(call(*operands))]
    sub x7 -> x0, other arithmetic: 13.1 us -> none  [the longest x1 11.6 us: vertical_mix(): denom = diagonal - below * ratios[-1]]
    ppermute x40 -> x0, waiting for transfers between devices: 13 us -> none  [the longest x8 7.36 us: extended_2(): after = lax.ppermute(first, axis, down)]
    div x2 -> x0, other arithmetic: 9.35 us -> none  [the longest x1 9.34 us: vertical_mix(): value = (source + below * values[-1]) / denom]
  transfers between devices with their start and end apart: 40 -> 0, of which waited for: 13 -> 0; matrix products, arithmetic and copies ran while one was open for 10% -> 0% of each run, Pallas kernels for 0% -> 0%
where the time goes in v1:
time: 30.2 us; the launch traced here: 30 us
  Pallas kernels  27.3 us (90%)
  local copies, waits for them, and re-layouts  2.04 us (7%)
  between operations  0.64 us (2%)
    pallas_call x1, Pallas kernels, body(): return tuple(call(*operands))  27.3 us
    unnamed x2, local copies, waits for them, and re-layouts  2.04 us

profile of v1, /device:TPU:1, one launch (start us, length us, event | category | flops | bytes accessed | tf_op | source)
XLA Modules:
  0.0 30.0 jit_solution(9656068376073625975)
XLA Ops:
  0.6 27.3 %shard_map.68 = (f32[2,16,48,288]{3,2,1,0:T(8,128)S(1)}, f32[48,288]{1,0:T(8,128)S(1)}) custom-call(f32[4,16,48,288]{3,2,1,0:T(8,128)} %ocean.1, f32[16]{0:T(128)} %thick.1, f32[48,288]{1,0:T(8,128)} %mixing.1, f32[48,288]{1,0:T(8,128)} %damping.1, s32[32,64]{1,0:T(8,128)} %blocks.1), custom_call_target="tpu_custom_call" | custom-call | tf_op jit(solution)/shard_map/pallas_call | solution.py:653
  27.9 1.4 %copy.9 = f32[2,16,48,288]{3,2,1,0:T(8,128)} copy(f32[2,16,48,288]{3,2,1,0:T(8,128)S(1)} %get-tuple-element.2) | data formatting | bytes 3538944
  29.4 0.6 %copy.10 = f32[48,288]{1,0:T(8,128)} copy(f32[48,288]{1,0:T(8,128)S(1)} %get-tuple-element.3) | data formatting | bytes 110592
